TPU v7x, 32 devices: a whole 2x2x4 slice. The times are simulated.
32 devices in a mesh: pb: 4 (over y, x), ka: 8 (over z, core).
Axes of the slice: x: 2, y: 2, z: 4, core: 2. Of those that a mesh axis runs over, the one named last changes fastest.
Arguments:
- queries: bfloat16 [4096, 2048], P(('pb', 'ka')), may hold values from -3 to 3
- keys: bfloat16 [4096, 2048], P(('pb', 'ka')), may hold values from -3 to 3
- values: bfloat16 [4096, 2048], P(('pb', 'ka')), may hold values from -3 to 3
- outputs: bfloat16 [4096, 2048], P(('pb', 'ka')), may hold values from -3 to 3
- d_out: bfloat16 [4096, 2048], P(('pb', 'ka')), may hold values from -16 to 16
- row_lse: float32 [16, 4096], P(None, ('pb', 'ka')), may hold values from 6.5 to 8.5
- adjacency: int32 [32, 2, 4, 1], P(('pb', 'ka')), may hold values from 0 to 1, as said below
Outputs:
- grad_queries: bfloat16 [4096, 2048], P(('pb', 'ka'))
- grad_keys: bfloat16 [4096, 2048], P(('pb', 'ka'))
- grad_values: bfloat16 [4096, 2048], P(('pb', 'ka'))
Inputs may be any that keep to these rules, and one draw needn't show every extreme that they name: 1 where the query block attends that key block of its window, else 0; every query block attends its own key block, adjacency[b, 0, 0, 0] = 1.
All inputs are finite; a program needn't handle non-finite values.
Results may differ from a plain program's by a relative error of at most 0.0075.
Values may be sent and summed in bfloat16 or wider, within the bound.
A program may use at most 128 MiB of HBM per device.

v0:
```python
import functools
import math

import jax
import jax.numpy as jnp
from jax import lax
from jax.experimental import pallas as pl
from jax.experimental.pallas import tpu as pltpu
from jax.sharding import PartitionSpec as P

HEAD_DIM = 128
BLOCK = 128
WINDOW = 4
GROUP_HEADS = 2
BIG = 1e30
MESH = pl.DeviceIdType.MESH

Q1, Q2, Q3, KV, R3, R2, R1, GKV = range(8)
KINDS = 8


def dot(a, b, da, db):
    return lax.dot_general(a, b, (((da,), (db,)), ((), ())), preferred_element_type=jnp.float32)


def kernel(
    rows, cols, groups, heads,
    q_ref, k_ref, v_ref, o_ref, do_ref, lse_ref, adj_ref,
    gq_out, gk_out, gv_out,
    visit, kvb, stats, gq_part, gkv_near, gq_send, gq_recv, gkv_send, gkv_recv,
    send_sem, recv_sem, stat_send, stat_recv,
):
    inverse = 1.0 / math.sqrt(HEAD_DIM)
    width = GROUP_HEADS * HEAD_DIM
    r = lax.axis_index("pb")
    c = lax.axis_index("ka")
    right = (r, lax.rem(c + 1, cols))
    left = (r, lax.rem(c + cols - 1, cols))
    below = (lax.rem(r + 1, rows), c)
    above = (lax.rem(r + rows - 1, rows), c)

    barrier = pltpu.get_barrier_semaphore()
    for other in (right, left, below, above):
        pl.semaphore_signal(barrier, inc=1, device_id=other, device_id_type=MESH)
    pl.semaphore_wait(barrier, 4)

    def message(kind, g):
        if kind in (Q1, Q2, Q3):
            src, dst, to = visit.at[kind, g], visit.at[kind + 1, g], right
        elif kind == KV:
            src = kvb.at[g, :, pl.ds(0, BLOCK), :]
            dst = kvb.at[g, :, pl.ds(BLOCK, BLOCK), :]
            to = above
        elif kind == GKV:
            src, dst, to = gkv_send.at[g], gkv_recv.at[g], below
        else:
            src, dst, to = gq_send.at[kind - R3, g], gq_recv.at[kind - R3, g], left
        return pltpu.make_async_remote_copy(
            src_ref=src, dst_ref=dst,
            send_sem=send_sem.at[kind, g], recv_sem=recv_sem.at[kind, g],
            device_id=to, device_id_type=MESH,
        )

    def stat_message(w):
        return pltpu.make_async_remote_copy(
            src_ref=stats.at[w], dst_ref=stats.at[w + 1],
            send_sem=stat_send.at[w], recv_sem=stat_recv.at[w],
            device_id=right, device_id_type=MESH,
        )

    def columns(g):
        return pl.ds(pl.multiple_of(g * width, width), width)

    def begin(g):
        here = columns(g)
        visit[0, g, 0] = q_ref[:, here]
        visit[0, g, 1] = do_ref[:, here]
        message(Q1, g).start()
        kvb[g, 0, pl.ds(0, BLOCK), :] = k_ref[:, here]
        kvb[g, 1, pl.ds(0, BLOCK), :] = v_ref[:, here]
        message(KV, g).start()

    def make_stats():
        ones = jnp.ones((8, HEAD_DIM), jnp.bfloat16)
        stats[0, pl.ds(0, heads), :] = lse_ref[...]
        for h in range(heads):
            part = pl.ds(h * HEAD_DIM, HEAD_DIM)
            product = do_ref[:, part].astype(jnp.float32) * o_ref[:, part].astype(jnp.float32)
            high = product.astype(jnp.bfloat16)
            low = (product - high.astype(jnp.float32)).astype(jnp.bfloat16)
            delta = dot(ones, high, 1, 1) + dot(ones, low, 1, 1)
            stats[0, pl.ds(heads + h, 1), :] = delta[0:1]
        for a in range(2):
            for w in range(WINDOW):
                blocked = (1 - adj_ref[0, a, w, 0]).astype(jnp.float32) * BIG
                stats[0, pl.ds(2 * heads + a * WINDOW + w, 1), :] = jnp.full((1, BLOCK), blocked, jnp.float32)

    def compute(g):
        for hh in range(GROUP_HEADS):
            h = g * GROUP_HEADS + hh
            part = slice(hh * HEAD_DIM, (hh + 1) * HEAD_DIM)
            kk = kvb[g, 0, :, part]
            vv = kvb[g, 1, :, part]
            qq = jnp.concatenate([visit[w, g, 0, :, part] for w in range(WINDOW)], axis=0)
            dd = jnp.concatenate([visit[w, g, 1, :, part] for w in range(WINDOW)], axis=0)
            delta = jnp.concatenate(
                [stats[w, pl.ds(heads + h, 1), :] for w in range(WINDOW)], axis=1
            )
            norms = [
                jnp.concatenate(
                    [
                        stats[w, pl.ds(h, 1), :] + stats[w, pl.ds(2 * heads + a * WINDOW + w, 1), :]
                        for w in range(WINDOW)
                    ],
                    axis=1,
                )
                for a in range(2)
            ]
            scores = dot(kk, qq, 1, 1) * inverse
            prob = jnp.concatenate(
                [jnp.exp(scores[:BLOCK] - norms[0]), jnp.exp(scores[BLOCK:] - norms[1])], axis=0
            )
            prob_grad = dot(vv, dd, 1, 1)
            score_grad = (prob * (prob_grad - delta) * inverse).astype(jnp.bfloat16)
            grad_v = dot(prob.astype(jnp.bfloat16), dd, 1, 0)
            grad_k = dot(score_grad, qq, 1, 0)
            grad_q = dot(score_grad, kk, 0, 0)
            gkv_near[g, 0, :, part] = grad_k[:BLOCK]
            gkv_near[g, 1, :, part] = grad_v[:BLOCK]
            gkv_send[g, 0, :, part] = grad_k[BLOCK:].astype(jnp.bfloat16)
            gkv_send[g, 1, :, part] = grad_v[BLOCK:].astype(jnp.bfloat16)
            for w in range(WINDOW - 1):
                gq_part[w, g, :, part] = grad_q[w * BLOCK : (w + 1) * BLOCK]
            gq_send[0, g, :, part] = grad_q[(WINDOW - 1) * BLOCK :].astype(jnp.bfloat16)

    def add_on(kind, g):
        step = kind - R3
        message(kind - 1, g).wait_recv()
        total = gq_recv[step - 1, g].astype(jnp.float32) + gq_part[WINDOW - 1 - step, g]
        gq_send[step, g] = total.astype(jnp.bfloat16)
        message(kind, g).start()

    def finish(g):
        here = columns(g)
        message(R1, g).wait_recv()
        total = gq_recv[2, g].astype(jnp.float32) + gq_part[0, g]
        gq_out[:, here] = total.astype(jnp.bfloat16)
        message(GKV, g).wait_recv()
        gk_out[:, here] = (gkv_near[g, 0] + gkv_recv[g, 0].astype(jnp.float32)).astype(jnp.bfloat16)
        gv_out[:, here] = (gkv_near[g, 1] + gkv_recv[g, 1].astype(jnp.float32)).astype(jnp.bfloat16)

    def at(i, skew, action):
        g = i - skew

        @pl.when((g >= 0) & (g < groups))
        def _():
            action(g)

    def forward(kind, g):
        message(kind - 1, g).wait_recv()
        message(kind, g).start()

    def work(g):
        message(Q3, g).wait_recv()
        message(KV, g).wait_recv()
        compute(g)
        message(R3, g).start()
        message(GKV, g).start()

    def turn(i, carry):
        at(i, 0, begin)

        @pl.when(i == 0)
        def _():
            make_stats()
            stat_message(0).start()

        for w in (1, 2):

            @pl.when(i == w)
            def _():
                stat_message(w - 1).wait_recv()
                stat_message(w).start()

        at(i, 1, functools.partial(forward, Q2))
        at(i, 2, functools.partial(forward, Q3))

        @pl.when(i == 3)
        def _():
            stat_message(2).wait_recv()

        at(i, 3, work)
        at(i, 4, functools.partial(add_on, R2))
        at(i, 5, functools.partial(add_on, R1))
        at(i, 6, finish)
        return carry

    lax.fori_loop(0, groups + 6, turn, 0)

    for w in range(WINDOW - 1):
        stat_message(w).wait_send()

    def drain(g, carry):
        for kind in range(KINDS):
            message(kind, g).wait_send()
        return carry

    lax.fori_loop(0, groups, drain, 0)


def local(rows, cols, queries, keys, values, outputs, d_out, row_lse, adjacency):
    tokens, features = queries.shape
    heads = features // HEAD_DIM
    groups = heads // GROUP_HEADS
    width = GROUP_HEADS * HEAD_DIM
    low, wide = jnp.bfloat16, jnp.float32
    vmem = pl.BlockSpec(memory_space=pltpu.VMEM)
    out = jax.ShapeDtypeStruct((tokens, features), low)
    pairs = 2 * WINDOW * heads
    return pl.pallas_call(
        functools.partial(kernel, rows, cols, groups, heads),
        out_shape=(out, out, out),
        in_specs=[vmem] * 6 + [pl.BlockSpec(memory_space=pltpu.SMEM)],
        out_specs=(vmem, vmem, vmem),
        scratch_shapes=[
            pltpu.VMEM((WINDOW, groups, 2, BLOCK, width), low),
            pltpu.VMEM((groups, 2, 2 * BLOCK, width), low),
            pltpu.VMEM((WINDOW, 2 * heads + 2 * WINDOW, BLOCK), wide),
            pltpu.VMEM((WINDOW - 1, groups, BLOCK, width), wide),
            pltpu.VMEM((groups, 2, BLOCK, width), wide),
            pltpu.VMEM((WINDOW - 1, groups, BLOCK, width), low),
            pltpu.VMEM((WINDOW - 1, groups, BLOCK, width), low),
            pltpu.VMEM((groups, 2, BLOCK, width), low),
            pltpu.VMEM((groups, 2, BLOCK, width), low),
            pltpu.SemaphoreType.DMA((KINDS, groups)),
            pltpu.SemaphoreType.DMA((KINDS, groups)),
            pltpu.SemaphoreType.DMA((WINDOW - 1,)),
            pltpu.SemaphoreType.DMA((WINDOW - 1,)),
        ],
        compiler_params=pltpu.CompilerParams(
            collective_id=0, has_side_effects=True, vmem_limit_bytes=48 * 1024 * 1024
        ),
        cost_estimate=pl.CostEstimate(
            flops=pairs * 5 * 2 * BLOCK * BLOCK * HEAD_DIM,
            bytes_accessed=8 * tokens * features * 2,
            transcendentals=pairs * BLOCK * BLOCK,
        ),
        name="block_sparse_backward",
    )(queries, keys, values, outputs, d_out, row_lse, adjacency)


def solution(mesh):
    token_rows = P(("pb", "ka"), None)
    placed = (token_rows,) * 5 + (P(None, ("pb", "ka")), P(("pb", "ka"), None, None, None))
    return jax.shard_map(
        functools.partial(local, mesh.shape["pb"], mesh.shape["ka"]),
        mesh=mesh,
        in_specs=placed,
        out_specs=(token_rows, token_rows, token_rows),
        check_vma=False,
    )
```

profile of v0, /device:TPU:0, one launch (start us, length us, event | category | flops | bytes accessed | tf_op | source)
XLA Modules:
  0.0 72.2 jit_solution(5232610301500572221)
XLA Ops:
  0.6 0.8 %copy.10.adj_ref = s32[1,2,4,1]{3,2,1,0:T(4,128)S(1)} copy(s32[1,2,4,1]{2,3,1,0:T(1,128)} %param.13) | data formatting | bytes 64 | tf_op args[6]
  1.4 0.0 copy-start
  1.4 1.0 %copy-done = bf16[128,2048]{1,0:T(8,128)(2,1)S(1)} copy-done((bf16[128,2048]{1,0:T(8,128)(2,1)S(1)}, bf16[128,2048]{1,0:T(8,128)(2,1)}, u32[]{:S(2)}) %copy-start) | copy-done | bytes 524312
  2.4 0.0 copy-start.1
  2.4 1.0 %copy-done.1 = bf16[128,2048]{1,0:T(8,128)(2,1)S(1)} copy-done((bf16[128,2048]{1,0:T(8,128)(2,1)S(1)}, bf16[128,2048]{1,0:T(8,128)(2,1)}, u32[]{:S(2)}) %copy-start.1) | copy-done | bytes 524312
  3.5 0.0 copy-start.2
  3.5 1.0 %copy-done.2 = bf16[128,2048]{1,0:T(8,128)(2,1)S(1)} copy-done((bf16[128,2048]{1,0:T(8,128)(2,1)S(1)}, bf16[128,2048]{1,0:T(8,128)(2,1)}, u32[]{:S(2)}) %copy-start.2) | copy-done | bytes 524312
  4.5 0.0 copy-start.3
  4.5 1.0 %copy-done.3 = bf16[128,2048]{1,0:T(8,128)(2,1)S(1)} copy-done((bf16[128,2048]{1,0:T(8,128)(2,1)S(1)}, bf16[128,2048]{1,0:T(8,128)(2,1)}, u32[]{:S(2)}) %copy-start.3) | copy-done | bytes 524312
  5.6 0.0 copy-start.4
  5.6 1.0 %copy-done.4 = bf16[128,2048]{1,0:T(8,128)(2,1)S(1)} copy-done((bf16[128,2048]{1,0:T(8,128)(2,1)S(1)}, bf16[128,2048]{1,0:T(8,128)(2,1)}, u32[]{:S(2)}) %copy-start.4) | copy-done | bytes 524312
  6.6 0.0 copy-start.5
  6.6 0.7 copy-done.5
  7.3 62.5 %block_sparse_backward.1 = (bf16[128,2048]{1,0:T(8,128)(2,1)S(1)}, bf16[128,2048]{1,0:T(8,128)(2,1)S(1)}, bf16[128,2048]{1,0:T(8,128)(2,1)S(1)}) custom-call(bf16[128,2048]{1,0:T(8,128)(2,1)S(1)} %copy-done, bf16[128,2048]{1,0:T(8,128)(2,1)S(1)} %copy-done.1, bf16[128,2048]{1,0:T(8,128)(2,1)S(1)} %copy-done.2, bf16[128,2048]{1,0:T(8,128)(2,1)S(1)} %copy-done.3, ...), custom_call_target="tpu_custom_call" | custom-call | flops 2684354560 | bytes 4194304 | tf_op jit(solution)/shard_map/block_sparse_backward/pallas_call | solution.py:220
  69.8 0.8 %copy.14 = bf16[128,2048]{1,0:T(8,128)(2,1)} copy(bf16[128,2048]{1,0:T(8,128)(2,1)S(1)} %get-tuple-element.6) | data formatting | bytes 1048576
  70.6 0.8 %copy.15 = bf16[128,2048]{1,0:T(8,128)(2,1)} copy(bf16[128,2048]{1,0:T(8,128)(2,1)S(1)} %get-tuple-element.7) | data formatting | bytes 1048576
  71.4 0.8 %copy.16 = bf16[128,2048]{1,0:T(8,128)(2,1)} copy(bf16[128,2048]{1,0:T(8,128)(2,1)S(1)} %get-tuple-element.8) | data formatting | bytes 1048576
Async XLA Ops:
  1.4 1.0 %copy-start = (bf16[128,2048]{1,0:T(8,128)(2,1)S(1)}, bf16[128,2048]{1,0:T(8,128)(2,1)}, u32[]{:S(2)}) copy-start(bf16[128,2048]{1,0:T(8,128)(2,1)} %q_ref.1) | copy-start | bytes 1572868
  2.4 1.0 %copy-start.1 = (bf16[128,2048]{1,0:T(8,128)(2,1)S(1)}, bf16[128,2048]{1,0:T(8,128)(2,1)}, u32[]{:S(2)}) copy-start(bf16[128,2048]{1,0:T(8,128)(2,1)} %k_ref.1) | copy-start | bytes 1572868
  3.5 1.0 %copy-start.2 = (bf16[128,2048]{1,0:T(8,128)(2,1)S(1)}, bf16[128,2048]{1,0:T(8,128)(2,1)}, u32[]{:S(2)}) copy-start(bf16[128,2048]{1,0:T(8,128)(2,1)} %v_ref.1) | copy-start | bytes 1572868
  4.5 1.0 %copy-start.3 = (bf16[128,2048]{1,0:T(8,128)(2,1)S(1)}, bf16[128,2048]{1,0:T(8,128)(2,1)}, u32[]{:S(2)}) copy-start(bf16[128,2048]{1,0:T(8,128)(2,1)} %o_ref.1) | copy-start | bytes 1572868
  5.6 1.0 %copy-start.4 = (bf16[128,2048]{1,0:T(8,128)(2,1)S(1)}, bf16[128,2048]{1,0:T(8,128)(2,1)}, u32[]{:S(2)}) copy-start(bf16[128,2048]{1,0:T(8,128)(2,1)} %do_ref.1) | copy-start | bytes 1572868
  6.6 0.7 copy-start.5
where the time goes:
time: 72.9 us; the launch traced here: 72.2 us
  Pallas kernels  62.5 us (86%)
  local copies, waits for them, and re-layouts  9.05 us (12%)
    pallas_call x1, Pallas kernels, local(): pl.pallas_call(functools.partial(kernel, rows, cols, groups, heads), out_...  62.5 us
    unnamed x16, local copies, waits for them, and re-layouts  9.05 us

commit v1 on v0

--- a/solution.py
+++ b/solution.py
@@ -11,7 +11,8 @@
 HEAD_DIM = 128
 BLOCK = 128
 WINDOW = 4
-GROUP_HEADS = 2
+GROUP_HEADS = 1
+AHEAD = 4
 BIG = 1e30
 MESH = pl.DeviceIdType.MESH
 
@@ -25,8 +26,9 @@
 
 def kernel(
     rows, cols, groups, heads,
-    q_ref, k_ref, v_ref, o_ref, do_ref, lse_ref, adj_ref,
+    q_hbm, k_hbm, v_hbm, o_hbm, do_hbm, lse_hbm, adj_ref,
     gq_out, gk_out, gv_out,
+    q_ref, k_ref, v_ref, o_ref, do_ref, lse_ref, load_sem, done, done_sem,
     visit, kvb, stats, gq_part, gkv_near, gq_send, gq_recv, gkv_send, gkv_recv,
     send_sem, recv_sem, stat_send, stat_recv,
 ):
@@ -38,6 +40,22 @@
     left = (r, lax.rem(c + cols - 1, cols))
     below = (lax.rem(r + 1, rows), c)
     above = (lax.rem(r + rows - 1, rows), c)
+
+    loads = [
+        pltpu.make_async_copy(source, target, load_sem.at[n])
+        for n, (source, target) in enumerate(
+            (
+                (q_hbm, q_ref),
+                (do_hbm, do_ref),
+                (k_hbm, k_ref),
+                (v_hbm, v_ref),
+                (o_hbm, o_ref),
+                (lse_hbm, lse_ref),
+            )
+        )
+    ]
+    for load in loads:
+        load.start()
 
     barrier = pltpu.get_barrier_semaphore()
     for other in (right, left, below, above):
@@ -92,7 +110,7 @@
             stats[0, pl.ds(heads + h, 1), :] = delta[0:1]
         for a in range(2):
             for w in range(WINDOW):
-                blocked = (1 - adj_ref[0, a, w, 0]).astype(jnp.float32) * BIG
+                blocked = (1 - adj_ref[0, a, 0, w]).astype(jnp.float32) * BIG
                 stats[0, pl.ds(2 * heads + a * WINDOW + w, 1), :] = jnp.full((1, BLOCK), blocked, jnp.float32)
 
     def compute(g):
@@ -140,14 +158,20 @@
         gq_send[step, g] = total.astype(jnp.bfloat16)
         message(kind, g).start()
 
+    def store(n, g):
+        out = (gq_out, gk_out, gv_out)[n]
+        return pltpu.make_async_copy(done.at[n, g], out.at[:, columns(g)], done_sem.at[n, g])
+
     def finish(g):
-        here = columns(g)
         message(R1, g).wait_recv()
         total = gq_recv[2, g].astype(jnp.float32) + gq_part[0, g]
-        gq_out[:, here] = total.astype(jnp.bfloat16)
+        done[0, g] = total.astype(jnp.bfloat16)
         message(GKV, g).wait_recv()
-        gk_out[:, here] = (gkv_near[g, 0] + gkv_recv[g, 0].astype(jnp.float32)).astype(jnp.bfloat16)
-        gv_out[:, here] = (gkv_near[g, 1] + gkv_recv[g, 1].astype(jnp.float32)).astype(jnp.bfloat16)
+        for n in range(2):
+            total = gkv_near[g, n] + gkv_recv[g, n].astype(jnp.float32)
+            done[n + 1, g] = total.astype(jnp.bfloat16)
+        for n in range(3):
+            store(n, g).start()
 
     def at(i, skew, action):
         g = i - skew
@@ -167,35 +191,44 @@
         message(R3, g).start()
         message(GKV, g).start()
 
+    def stats_forward(w):
+        stat_message(w - 1).wait_recv()
+        stat_message(w).start()
+
     def turn(i, carry):
-        at(i, 0, begin)
+        at(i, -AHEAD, begin)
+        at(i, 0, functools.partial(forward, Q2))
 
         @pl.when(i == 0)
         def _():
-            make_stats()
-            stat_message(0).start()
-
-        for w in (1, 2):
-
-            @pl.when(i == w)
-            def _():
-                stat_message(w - 1).wait_recv()
-                stat_message(w).start()
-
-        at(i, 1, functools.partial(forward, Q2))
+            stats_forward(1)
+
         at(i, 2, functools.partial(forward, Q3))
 
-        @pl.when(i == 3)
+        @pl.when(i == 2)
+        def _():
+            stats_forward(2)
+
+        @pl.when(i == 4)
         def _():
             stat_message(2).wait_recv()
 
-        at(i, 3, work)
-        at(i, 4, functools.partial(add_on, R2))
-        at(i, 5, functools.partial(add_on, R1))
-        at(i, 6, finish)
+        at(i, 4, work)
+        at(i, 6, functools.partial(add_on, R2))
+        at(i, 8, functools.partial(add_on, R1))
+        at(i, 10, finish)
         return carry
 
-    lax.fori_loop(0, groups + 6, turn, 0)
+    for load in loads[:4]:
+        load.wait()
+    for g in range(AHEAD):
+        begin(g)
+    for load in loads[4:]:
+        load.wait()
+    make_stats()
+    stat_message(0).start()
+
+    lax.fori_loop(0, groups + 10, turn, 0)
 
     for w in range(WINDOW - 1):
         stat_message(w).wait_send()
@@ -203,9 +236,22 @@
     def drain(g, carry):
         for kind in range(KINDS):
             message(kind, g).wait_send()
+        for n in range(3):
+            store(n, g).wait()
         return carry
 
     lax.fori_loop(0, groups, drain, 0)
+
+
+def store_kernel(a_ref, b_ref, c_ref, a_out, b_out, c_out, sem):
+    stores = [
+        pltpu.make_async_copy(source, target, sem.at[n])
+        for n, (source, target) in enumerate(((a_ref, a_out), (b_ref, b_out), (c_ref, c_out)))
+    ]
+    for store in stores:
+        store.start()
+    for store in stores:
+        store.wait()
 
 
 def local(rows, cols, queries, keys, values, outputs, d_out, row_lse, adjacency):
@@ -214,15 +260,20 @@
     groups = heads // GROUP_HEADS
     width = GROUP_HEADS * HEAD_DIM
     low, wide = jnp.bfloat16, jnp.float32
-    vmem = pl.BlockSpec(memory_space=pltpu.VMEM)
+    hbm = pl.BlockSpec(memory_space=pltpu.HBM)
     out = jax.ShapeDtypeStruct((tokens, features), low)
     pairs = 2 * WINDOW * heads
-    return pl.pallas_call(
+    grads = pl.pallas_call(
         functools.partial(kernel, rows, cols, groups, heads),
         out_shape=(out, out, out),
-        in_specs=[vmem] * 6 + [pl.BlockSpec(memory_space=pltpu.SMEM)],
-        out_specs=(vmem, vmem, vmem),
-        scratch_shapes=[
+        in_specs=[hbm] * 6 + [pl.BlockSpec(memory_space=pltpu.SMEM)],
+        out_specs=(hbm, hbm, hbm),
+        scratch_shapes=[pltpu.VMEM((tokens, features), low)] * 5
+        + [
+            pltpu.VMEM((heads, tokens), wide),
+            pltpu.SemaphoreType.DMA((6,)),
+            pltpu.VMEM((3, groups, BLOCK, width), low),
+            pltpu.SemaphoreType.DMA((3, groups)),
             pltpu.VMEM((WINDOW, groups, 2, BLOCK, width), low),
             pltpu.VMEM((groups, 2, 2 * BLOCK, width), low),
             pltpu.VMEM((WINDOW, 2 * heads + 2 * WINDOW, BLOCK), wide),
@@ -238,7 +289,7 @@
             pltpu.SemaphoreType.DMA((WINDOW - 1,)),
         ],
         compiler_params=pltpu.CompilerParams(
-            collective_id=0, has_side_effects=True, vmem_limit_bytes=48 * 1024 * 1024
+            collective_id=0, has_side_effects=True, vmem_limit_bytes=62 * 1024 * 1024
         ),
         cost_estimate=pl.CostEstimate(
             flops=pairs * 5 * 2 * BLOCK * BLOCK * HEAD_DIM,
@@ -246,7 +297,16 @@
             transcendentals=pairs * BLOCK * BLOCK,
         ),
         name="block_sparse_backward",
-    )(queries, keys, values, outputs, d_out, row_lse, adjacency)
+    )(queries, keys, values, outputs, d_out, row_lse, adjacency.transpose(0, 1, 3, 2))
+    return pl.pallas_call(
+        store_kernel,
+        out_shape=(out, out, out),
+        in_specs=[hbm] * 3,
+        out_specs=(hbm, hbm, hbm),
+        scratch_shapes=[pltpu.SemaphoreType.DMA((3,))],
+        compiler_params=pltpu.CompilerParams(vmem_limit_bytes=62 * 1024 * 1024),
+        name="store_gradients",
+    )(*grads)
 
 
 def solution(mesh):

time: 72.9 us -> 116 us (1.59)
  Pallas kernels: 62.5 us -> 114 us
  local copies, waits for them, and re-layouts: 9.05 us -> 0 us
    pallas_call x0 -> x1, Pallas kernels: none -> 48.8 us  [local(): pl.pallas_call(store_kernel, out_shape=(out, out, out), in_specs=[hbm] *...]
    unnamed x16 -> x0, local copies, waits for them, and re-layouts: 9.05 us -> none
    pallas_call x1, Pallas kernels: 62.5 us -> 64.9 us  [local(): pl.pallas_call(functools.partial(kernel, rows, cols, groups, heads), out_...]
where the time goes in v1:
time: 116 us; the launch traced here: 114 us
  Pallas kernels  114 us (98%)
    pallas_call x1, Pallas kernels, local(): pl.pallas_call(functools.partial(kernel, rows, cols, groups, heads), out_...  64.9 us
    pallas_call x1, Pallas kernels, local(): pl.pallas_call(store_kernel, out_shape=(out, out, out), in_specs=[hbm] *...  48.8 us

profile of v1, /device:TPU:0, one launch (start us, length us, event | category | flops | bytes accessed | tf_op | source)
XLA Modules:
  0.0 114.3 jit_solution(924967874757770998)
XLA Ops:
  0.6 64.9 %block_sparse_backward.1 = (bf16[128,2048]{1,0:T(8,128)(2,1)}, bf16[128,2048]{1,0:T(8,128)(2,1)}, bf16[128,2048]{1,0:T(8,128)(2,1)}) custom-call(bf16[128,2048]{1,0:T(8,128)(2,1)} %q_hbm.1, bf16[128,2048]{1,0:T(8,128)(2,1)} %k_hbm.1, bf16[128,2048]{1,0:T(8,128)(2,1)} %v_hbm.1, bf16[128,2048]{1,0:T(8,128)(2,1)} %o_hbm.1, bf16[128,2048]{1,0:T(8,128)(2,1)} %do_hbm.1, ...), custom_call_target="tpu_custom_call" | custom-call | flops 2684354560 | bytes 4194304 | tf_op jit(solution)/shard_map/block_sparse_backward/pallas_call | solution.py:266
  65.5 48.8 %store_gradients.1 = (bf16[128,2048]{1,0:T(8,128)(2,1)}, bf16[128,2048]{1,0:T(8,128)(2,1)}, bf16[128,2048]{1,0:T(8,128)(2,1)}) custom-call(bf16[128,2048]{1,0:T(8,128)(2,1)} %get-tuple-element.6.a_ref, bf16[128,2048]{1,0:T(8,128)(2,1)} %get-tuple-element.7.b_ref, bf16[128,2048]{1,0:T(8,128)(2,1)} %get-tuple-element.8.c_ref), custom_call_target="tpu_custom_call" | custom-call | tf_op jit(solution)/shard_map/store_gradients/pallas_call | solution.py:301

commit v2 on v1

--- a/solution.py
+++ b/solution.py
@@ -12,7 +12,7 @@
 BLOCK = 128
 WINDOW = 4
 GROUP_HEADS = 1
-AHEAD = 4
+AHEAD = 8
 BIG = 1e30
 MESH = pl.DeviceIdType.MESH
 
@@ -89,11 +89,14 @@
     def columns(g):
         return pl.ds(pl.multiple_of(g * width, width), width)
 
-    def begin(g):
+    def begin_queries(g):
         here = columns(g)
         visit[0, g, 0] = q_ref[:, here]
         visit[0, g, 1] = do_ref[:, here]
         message(Q1, g).start()
+
+    def begin_keys(g):
+        here = columns(g)
         kvb[g, 0, pl.ds(0, BLOCK), :] = k_ref[:, here]
         kvb[g, 1, pl.ds(0, BLOCK), :] = v_ref[:, here]
         message(KV, g).start()
@@ -172,6 +175,12 @@
             done[n + 1, g] = total.astype(jnp.bfloat16)
         for n in range(3):
             store(n, g).start()
+        for kind in range(KINDS):
+            message(kind, g).wait_send()
+
+    def settle(g):
+        for n in range(3):
+            store(n, g).wait()
 
     def at(i, skew, action):
         g = i - skew
@@ -196,7 +205,8 @@
         stat_message(w).start()
 
     def turn(i, carry):
-        at(i, -AHEAD, begin)
+        at(i, -AHEAD, begin_queries)
+        at(i, -AHEAD, begin_keys)
         at(i, 0, functools.partial(forward, Q2))
 
         @pl.when(i == 0)
@@ -217,38 +227,44 @@
         at(i, 6, functools.partial(add_on, R2))
         at(i, 8, functools.partial(add_on, R1))
         at(i, 10, finish)
+        at(i, 12, settle)
         return carry
 
-    for load in loads[:4]:
+    for load in loads[:2]:
         load.wait()
     for g in range(AHEAD):
-        begin(g)
+        begin_queries(g)
+    for load in loads[2:4]:
+        load.wait()
+    for g in range(AHEAD):
+        begin_keys(g)
     for load in loads[4:]:
         load.wait()
     make_stats()
     stat_message(0).start()
 
-    lax.fori_loop(0, groups + 10, turn, 0)
+    lax.fori_loop(0, groups + 12, turn, 0)
 
     for w in range(WINDOW - 1):
         stat_message(w).wait_send()
 
-    def drain(g, carry):
-        for kind in range(KINDS):
-            message(kind, g).wait_send()
-        for n in range(3):
-            store(n, g).wait()
-        return carry
-
-    lax.fori_loop(0, groups, drain, 0)
-
-
-def store_kernel(a_ref, b_ref, c_ref, a_out, b_out, c_out, sem):
+
+def store_kernel(a_ref, b_ref, c_ref, a_out, b_out, c_out, held, in_sem, out_sem):
+    half = a_ref.shape[0] // 2
+    refs = ((a_ref, a_out), (b_ref, b_out), (c_ref, c_out))
+    pieces = [(n, p, pl.ds(p * half, half)) for p in range(2) for n in range(3)]
+    fetches = [
+        pltpu.make_async_copy(refs[n][0].at[here], held.at[n, here], in_sem.at[n, p])
+        for n, p, here in pieces
+    ]
     stores = [
-        pltpu.make_async_copy(source, target, sem.at[n])
-        for n, (source, target) in enumerate(((a_ref, a_out), (b_ref, b_out), (c_ref, c_out)))
+        pltpu.make_async_copy(held.at[n, here], refs[n][1].at[here], out_sem.at[n, p])
+        for n, p, here in pieces
     ]
-    for store in stores:
+    for fetch in fetches:
+        fetch.start()
+    for fetch, store in zip(fetches, stores):
+        fetch.wait()
         store.start()
     for store in stores:
         store.wait()
@@ -303,7 +319,11 @@
         out_shape=(out, out, out),
         in_specs=[hbm] * 3,
         out_specs=(hbm, hbm, hbm),
-        scratch_shapes=[pltpu.SemaphoreType.DMA((3,))],
+        scratch_shapes=[
+            pltpu.VMEM((3, tokens, features), low),
+            pltpu.SemaphoreType.DMA((3, 2)),
+            pltpu.SemaphoreType.DMA((3, 2)),
+        ],
         compiler_params=pltpu.CompilerParams(vmem_limit_bytes=62 * 1024 * 1024),
         name="store_gradients",
     )(*grads)

time: 116 us -> 68.9 us (0.59)
  Pallas kernels: 114 us -> 67.4 us
    pallas_call x1, Pallas kernels: 48.8 us -> 2.19 us  [local(): pl.pallas_call(store_kernel, out_shape=(out, out, out), in_specs=[hbm] *...]
where the time goes in v2:
time: 68.9 us; the launch traced here: 68 us
  Pallas kernels  67.4 us (98%)
    pallas_call x1, Pallas kernels, local(): pl.pallas_call(functools.partial(kernel, rows, cols, groups, heads), out_...  65.2 us
    pallas_call x1, Pallas kernels, local(): pl.pallas_call(store_kernel, out_shape=(out, out, out), in_specs=[hbm] *...  2.19 us

profile of v2, /device:TPU:0, one launch (start us, length us, event | category | flops | bytes accessed | tf_op | source)
XLA Modules:
  0.0 68.0 jit_solution(17507453792734342305)
XLA Ops:
  0.6 65.2 %block_sparse_backward.1 = (bf16[128,2048]{1,0:T(8,128)(2,1)}, bf16[128,2048]{1,0:T(8,128)(2,1)}, bf16[128,2048]{1,0:T(8,128)(2,1)}) custom-call(bf16[128,2048]{1,0:T(8,128)(2,1)} %q_hbm.1, bf16[128,2048]{1,0:T(8,128)(2,1)} %k_hbm.1, bf16[128,2048]{1,0:T(8,128)(2,1)} %v_hbm.1, bf16[128,2048]{1,0:T(8,128)(2,1)} %o_hbm.1, bf16[128,2048]{1,0:T(8,128)(2,1)} %do_hbm.1, ...), custom_call_target="tpu_custom_call" | custom-call | flops 2684354560 | bytes 4194304 | tf_op jit(solution)/shard_map/block_sparse_backward/pallas_call | solution.py:282
  65.8 2.2 %store_gradients.1 = (bf16[128,2048]{1,0:T(8,128)(2,1)}, bf16[128,2048]{1,0:T(8,128)(2,1)}, bf16[128,2048]{1,0:T(8,128)(2,1)}) custom-call(bf16[128,2048]{1,0:T(8,128)(2,1)} %get-tuple-element.6.a_ref, bf16[128,2048]{1,0:T(8,128)(2,1)} %get-tuple-element.7.b_ref, bf16[128,2048]{1,0:T(8,128)(2,1)} %get-tuple-element.8.c_ref), custom_call_target="tpu_custom_call" | custom-call | tf_op jit(solution)/shard_map/store_gradients/pallas_call | solution.py:317

commit v3 on v2

--- a/solution.py
+++ b/solution.py
@@ -11,8 +11,7 @@
 HEAD_DIM = 128
 BLOCK = 128
 WINDOW = 4
-GROUP_HEADS = 1
-AHEAD = 8
+AHEAD = 4
 BIG = 1e30
 MESH = pl.DeviceIdType.MESH
 
@@ -29,11 +28,11 @@
     q_hbm, k_hbm, v_hbm, o_hbm, do_hbm, lse_hbm, adj_ref,
     gq_out, gk_out, gv_out,
     q_ref, k_ref, v_ref, o_ref, do_ref, lse_ref, load_sem, done, done_sem,
-    visit, kvb, stats, gq_part, gkv_near, gq_send, gq_recv, gkv_send, gkv_recv,
+    visit, kvb, stats, probs, score_grads, gq_part, gkv_near, gq_send, gq_recv, gkv_send, gkv_recv,
     send_sem, recv_sem, stat_send, stat_recv,
 ):
     inverse = 1.0 / math.sqrt(HEAD_DIM)
-    width = GROUP_HEADS * HEAD_DIM
+    width = HEAD_DIM
     r = lax.axis_index("pb")
     c = lax.axis_index("ka")
     right = (r, lax.rem(c + 1, cols))
@@ -116,43 +115,48 @@
                 blocked = (1 - adj_ref[0, a, 0, w]).astype(jnp.float32) * BIG
                 stats[0, pl.ds(2 * heads + a * WINDOW + w, 1), :] = jnp.full((1, BLOCK), blocked, jnp.float32)
 
-    def compute(g):
-        for hh in range(GROUP_HEADS):
-            h = g * GROUP_HEADS + hh
-            part = slice(hh * HEAD_DIM, (hh + 1) * HEAD_DIM)
-            kk = kvb[g, 0, :, part]
-            vv = kvb[g, 1, :, part]
-            qq = jnp.concatenate([visit[w, g, 0, :, part] for w in range(WINDOW)], axis=0)
-            dd = jnp.concatenate([visit[w, g, 1, :, part] for w in range(WINDOW)], axis=0)
-            delta = jnp.concatenate(
-                [stats[w, pl.ds(heads + h, 1), :] for w in range(WINDOW)], axis=1
+    def pair_terms(g, first):
+        pair = (first, first + 1)
+        span = pl.ds(first * BLOCK, 2 * BLOCK)
+        kk = kvb[g, 0]
+        vv = kvb[g, 1]
+        qq = visit[first : first + 2, g, 0].reshape(2 * BLOCK, HEAD_DIM)
+        dd = visit[first : first + 2, g, 1].reshape(2 * BLOCK, HEAD_DIM)
+        delta = jnp.concatenate([stats[w, pl.ds(heads + g, 1), :] for w in pair], axis=1)
+        for a in range(2):
+            norms = jnp.concatenate(
+                [
+                    stats[w, pl.ds(g, 1), :] + stats[w, pl.ds(2 * heads + a * WINDOW + w, 1), :]
+                    for w in pair
+                ],
+                axis=1,
             )
-            norms = [
-                jnp.concatenate(
-                    [
-                        stats[w, pl.ds(h, 1), :] + stats[w, pl.ds(2 * heads + a * WINDOW + w, 1), :]
-                        for w in range(WINDOW)
-                    ],
-                    axis=1,
-                )
-                for a in range(2)
-            ]
-            scores = dot(kk, qq, 1, 1) * inverse
-            prob = jnp.concatenate(
-                [jnp.exp(scores[:BLOCK] - norms[0]), jnp.exp(scores[BLOCK:] - norms[1])], axis=0
-            )
-            prob_grad = dot(vv, dd, 1, 1)
-            score_grad = (prob * (prob_grad - delta) * inverse).astype(jnp.bfloat16)
-            grad_v = dot(prob.astype(jnp.bfloat16), dd, 1, 0)
-            grad_k = dot(score_grad, qq, 1, 0)
-            grad_q = dot(score_grad, kk, 0, 0)
-            gkv_near[g, 0, :, part] = grad_k[:BLOCK]
-            gkv_near[g, 1, :, part] = grad_v[:BLOCK]
-            gkv_send[g, 0, :, part] = grad_k[BLOCK:].astype(jnp.bfloat16)
-            gkv_send[g, 1, :, part] = grad_v[BLOCK:].astype(jnp.bfloat16)
-            for w in range(WINDOW - 1):
-                gq_part[w, g, :, part] = grad_q[w * BLOCK : (w + 1) * BLOCK]
-            gq_send[0, g, :, part] = grad_q[(WINDOW - 1) * BLOCK :].astype(jnp.bfloat16)
+            half = slice(a * BLOCK, (a + 1) * BLOCK)
+            prob = jnp.exp(dot(kk[half], qq, 1, 1) * inverse - norms)
+            probs[g, half, span] = prob.astype(jnp.bfloat16)
+            prob_grad = dot(vv[half], dd, 1, 1)
+            score_grad = prob * (prob_grad - delta) * inverse
+            score_grads[g, half, span] = score_grad.astype(jnp.bfloat16)
+        return dot(score_grads[g, :, span], kk, 0, 0)
+
+    def work_near(g):
+        message(KV, g).wait_recv()
+        grad_q = pair_terms(g, 0)
+        gq_part[0, g] = grad_q[:BLOCK]
+        gq_part[1, g] = grad_q[BLOCK:]
+
+    def work_far(g):
+        message(Q3, g).wait_recv()
+        grad_q = pair_terms(g, 2)
+        gq_part[2, g] = grad_q[:BLOCK]
+        gq_send[0, g] = grad_q[BLOCK:].astype(jnp.bfloat16)
+        message(R3, g).start()
+        qq = visit[:, g, 0].reshape(WINDOW * BLOCK, HEAD_DIM)
+        dd = visit[:, g, 1].reshape(WINDOW * BLOCK, HEAD_DIM)
+        for n, total in ((0, dot(score_grads[g], qq, 1, 0)), (1, dot(probs[g], dd, 1, 0))):
+            gkv_near[g, n] = total[:BLOCK]
+            gkv_send[g, n] = total[BLOCK:].astype(jnp.bfloat16)
+        message(GKV, g).start()
 
     def add_on(kind, g):
         step = kind - R3
@@ -193,13 +197,6 @@
         message(kind - 1, g).wait_recv()
         message(kind, g).start()
 
-    def work(g):
-        message(Q3, g).wait_recv()
-        message(KV, g).wait_recv()
-        compute(g)
-        message(R3, g).start()
-        message(GKV, g).start()
-
     def stats_forward(w):
         stat_message(w - 1).wait_recv()
         stat_message(w).start()
@@ -213,6 +210,7 @@
         def _():
             stats_forward(1)
 
+        at(i, 1, work_near)
         at(i, 2, functools.partial(forward, Q3))
 
         @pl.when(i == 2)
@@ -223,7 +221,7 @@
         def _():
             stat_message(2).wait_recv()
 
-        at(i, 4, work)
+        at(i, 4, work_far)
         at(i, 6, functools.partial(add_on, R2))
         at(i, 8, functools.partial(add_on, R1))
         at(i, 10, finish)
@@ -273,8 +271,8 @@
 def local(rows, cols, queries, keys, values, outputs, d_out, row_lse, adjacency):
     tokens, features = queries.shape
     heads = features // HEAD_DIM
-    groups = heads // GROUP_HEADS
-    width = GROUP_HEADS * HEAD_DIM
+    groups = heads
+    width = HEAD_DIM
     low, wide = jnp.bfloat16, jnp.float32
     hbm = pl.BlockSpec(memory_space=pltpu.HBM)
     out = jax.ShapeDtypeStruct((tokens, features), low)
@@ -293,6 +291,8 @@
             pltpu.VMEM((WINDOW, groups, 2, BLOCK, width), low),
             pltpu.VMEM((groups, 2, 2 * BLOCK, width), low),
             pltpu.VMEM((WINDOW, 2 * heads + 2 * WINDOW, BLOCK), wide),
+            pltpu.VMEM((groups, 2 * BLOCK, WINDOW * BLOCK), low),
+            pltpu.VMEM((groups, 2 * BLOCK, WINDOW * BLOCK), low),
             pltpu.VMEM((WINDOW - 1, groups, BLOCK, width), wide),
             pltpu.VMEM((groups, 2, BLOCK, width), wide),
             pltpu.VMEM((WINDOW - 1, groups, BLOCK, width), low),

time: 68.9 us -> 68.8 us (level)
  no operation moved by 1% of the time
where the time goes in v3:
time: 68.8 us; the launch traced here: 67.9 us
  Pallas kernels  67.3 us (98%)
    pallas_call x1, Pallas kernels, local(): pl.pallas_call(functools.partial(kernel, rows, cols, groups, heads), out_...  65.1 us
    pallas_call x1, Pallas kernels, local(): pl.pallas_call(store_kernel, out_shape=(out, out, out), in_specs=[hbm] *...  2.19 us

profile of v3, /device:TPU:0, one launch (start us, length us, event | category | flops | bytes accessed | tf_op | source)
XLA Modules:
  0.0 67.9 jit_solution(1243945414503694550)
XLA Ops:
  0.6 65.1 %block_sparse_backward.1 = (bf16[128,2048]{1,0:T(8,128)(2,1)}, bf16[128,2048]{1,0:T(8,128)(2,1)}, bf16[128,2048]{1,0:T(8,128)(2,1)}) custom-call(bf16[128,2048]{1,0:T(8,128)(2,1)} %q_hbm.1, bf16[128,2048]{1,0:T(8,128)(2,1)} %k_hbm.1, bf16[128,2048]{1,0:T(8,128)(2,1)} %v_hbm.1, bf16[128,2048]{1,0:T(8,128)(2,1)} %o_hbm.1, bf16[128,2048]{1,0:T(8,128)(2,1)} %do_hbm.1, ...), custom_call_target="tpu_custom_call" | custom-call | flops 2684354560 | bytes 4194304 | tf_op jit(solution)/shard_map/block_sparse_backward/pallas_call | solution.py:280
  65.7 2.2 %store_gradients.1 = (bf16[128,2048]{1,0:T(8,128)(2,1)}, bf16[128,2048]{1,0:T(8,128)(2,1)}, bf16[128,2048]{1,0:T(8,128)(2,1)}) custom-call(bf16[128,2048]{1,0:T(8,128)(2,1)} %get-tuple-element.6.a_ref, bf16[128,2048]{1,0:T(8,128)(2,1)} %get-tuple-element.7.b_ref, bf16[128,2048]{1,0:T(8,128)(2,1)} %get-tuple-element.8.c_ref), custom_call_target="tpu_custom_call" | custom-call | tf_op jit(solution)/shard_map/store_gradients/pallas_call | solution.py:317

commit v4 on v3

--- a/solution.py
+++ b/solution.py
@@ -11,7 +11,7 @@
 HEAD_DIM = 128
 BLOCK = 128
 WINDOW = 4
-AHEAD = 4
+AHEAD = 8
 BIG = 1e30
 MESH = pl.DeviceIdType.MESH
 
@@ -29,7 +29,7 @@
     gq_out, gk_out, gv_out,
     q_ref, k_ref, v_ref, o_ref, do_ref, lse_ref, load_sem, done, done_sem,
     visit, kvb, stats, probs, score_grads, gq_part, gkv_near, gq_send, gq_recv, gkv_send, gkv_recv,
-    send_sem, recv_sem, stat_send, stat_recv,
+    send_sem, recv_sem, stat_send, stat_recv, gq_leap, leap_send, leap_recv,
 ):
     inverse = 1.0 / math.sqrt(HEAD_DIM)
     width = HEAD_DIM
@@ -39,15 +39,24 @@
     left = (r, lax.rem(c + cols - 1, cols))
     below = (lax.rem(r + 1, rows), c)
     above = (lax.rem(r + rows - 1, rows), c)
-
+    leaps = c == cols - (WINDOW - 1)
+    lands = c == 0
+    skips = c == cols - 1
+    leap_to = (r, 0)
+    leap_from = (r, cols - (WINDOW - 1))
+
+    ahead = pl.ds(0, AHEAD * width)
+    rest = pl.ds(AHEAD * width, (groups - AHEAD) * width)
     loads = [
         pltpu.make_async_copy(source, target, load_sem.at[n])
         for n, (source, target) in enumerate(
             (
-                (q_hbm, q_ref),
-                (do_hbm, do_ref),
+                (q_hbm.at[:, ahead], q_ref.at[:, ahead]),
+                (do_hbm.at[:, ahead], do_ref.at[:, ahead]),
                 (k_hbm, k_ref),
                 (v_hbm, v_ref),
+                (q_hbm.at[:, rest], q_ref.at[:, rest]),
+                (do_hbm.at[:, rest], do_ref.at[:, rest]),
                 (o_hbm, o_ref),
                 (lse_hbm, lse_ref),
             )
@@ -59,7 +68,22 @@
     barrier = pltpu.get_barrier_semaphore()
     for other in (right, left, below, above):
         pl.semaphore_signal(barrier, inc=1, device_id=other, device_id_type=MESH)
-    pl.semaphore_wait(barrier, 4)
+
+    @pl.when(leaps)
+    def _():
+        pl.semaphore_signal(barrier, inc=1, device_id=leap_to, device_id_type=MESH)
+
+    @pl.when(lands)
+    def _():
+        pl.semaphore_signal(barrier, inc=1, device_id=leap_from, device_id_type=MESH)
+
+    @pl.when(leaps | lands)
+    def _():
+        pl.semaphore_wait(barrier, 5)
+
+    @pl.when(jnp.logical_not(leaps | lands))
+    def _():
+        pl.semaphore_wait(barrier, 4)
 
     def message(kind, g):
         if kind in (Q1, Q2, Q3):
@@ -78,6 +102,20 @@
             device_id=to, device_id_type=MESH,
         )
 
+    def leap_query(g):
+        return pltpu.make_async_remote_copy(
+            src_ref=visit.at[0, g], dst_ref=visit.at[WINDOW - 1, g],
+            send_sem=leap_send.at[g], recv_sem=recv_sem.at[Q3, g],
+            device_id=leap_to, device_id_type=MESH,
+        )
+
+    def leap_gradient(g):
+        return pltpu.make_async_remote_copy(
+            src_ref=gq_send.at[0, g], dst_ref=gq_leap.at[g],
+            send_sem=send_sem.at[R3, g], recv_sem=leap_recv.at[g],
+            device_id=leap_from, device_id_type=MESH,
+        )
+
     def stat_message(w):
         return pltpu.make_async_remote_copy(
             src_ref=stats.at[w], dst_ref=stats.at[w + 1],
@@ -93,6 +131,10 @@
         visit[0, g, 0] = q_ref[:, here]
         visit[0, g, 1] = do_ref[:, here]
         message(Q1, g).start()
+
+        @pl.when(leaps)
+        def _():
+            leap_query(g).start()
 
     def begin_keys(g):
         here = columns(g)
@@ -150,7 +192,15 @@
         grad_q = pair_terms(g, 2)
         gq_part[2, g] = grad_q[:BLOCK]
         gq_send[0, g] = grad_q[BLOCK:].astype(jnp.bfloat16)
-        message(R3, g).start()
+
+        @pl.when(lands)
+        def _():
+            leap_gradient(g).start()
+
+        @pl.when(jnp.logical_not(lands))
+        def _():
+            message(R3, g).start()
+
         qq = visit[:, g, 0].reshape(WINDOW * BLOCK, HEAD_DIM)
         dd = visit[:, g, 1].reshape(WINDOW * BLOCK, HEAD_DIM)
         for n, total in ((0, dot(score_grads[g], qq, 1, 0)), (1, dot(probs[g], dd, 1, 0))):
@@ -158,12 +208,24 @@
             gkv_send[g, n] = total[BLOCK:].astype(jnp.bfloat16)
         message(GKV, g).start()
 
-    def add_on(kind, g):
-        step = kind - R3
-        message(kind - 1, g).wait_recv()
-        total = gq_recv[step - 1, g].astype(jnp.float32) + gq_part[WINDOW - 1 - step, g]
-        gq_send[step, g] = total.astype(jnp.bfloat16)
-        message(kind, g).start()
+    def add_second(g):
+        @pl.when(skips)
+        def _():
+            gq_send[1, g] = gq_part[2, g].astype(jnp.bfloat16)
+
+        @pl.when(jnp.logical_not(skips))
+        def _():
+            message(R3, g).wait_recv()
+            total = gq_recv[0, g].astype(jnp.float32) + gq_part[2, g]
+            gq_send[1, g] = total.astype(jnp.bfloat16)
+
+        message(R2, g).start()
+
+    def add_first(g):
+        message(R2, g).wait_recv()
+        total = gq_recv[1, g].astype(jnp.float32) + gq_part[1, g]
+        gq_send[2, g] = total.astype(jnp.bfloat16)
+        message(R1, g).start()
 
     def store(n, g):
         out = (gq_out, gk_out, gv_out)[n]
@@ -172,7 +234,16 @@
     def finish(g):
         message(R1, g).wait_recv()
         total = gq_recv[2, g].astype(jnp.float32) + gq_part[0, g]
-        done[0, g] = total.astype(jnp.bfloat16)
+
+        @pl.when(leaps)
+        def _():
+            leap_gradient(g).wait_recv()
+            done[0, g] = (total + gq_leap[g].astype(jnp.float32)).astype(jnp.bfloat16)
+
+        @pl.when(jnp.logical_not(leaps))
+        def _():
+            done[0, g] = total.astype(jnp.bfloat16)
+
         message(GKV, g).wait_recv()
         for n in range(2):
             total = gkv_near[g, n] + gkv_recv[g, n].astype(jnp.float32)
@@ -180,7 +251,16 @@
         for n in range(3):
             store(n, g).start()
         for kind in range(KINDS):
-            message(kind, g).wait_send()
+            if kind != Q3:
+                message(kind, g).wait_send()
+
+        @pl.when(jnp.logical_not(skips))
+        def _():
+            message(Q3, g).wait_send()
+
+        @pl.when(leaps)
+        def _():
+            leap_query(g).wait_send()
 
     def settle(g):
         for n in range(3):
@@ -193,9 +273,16 @@
         def _():
             action(g)
 
-    def forward(kind, g):
-        message(kind - 1, g).wait_recv()
-        message(kind, g).start()
+    def forward_first(g):
+        message(Q1, g).wait_recv()
+        message(Q2, g).start()
+
+    def forward_second(g):
+        message(Q2, g).wait_recv()
+
+        @pl.when(jnp.logical_not(skips))
+        def _():
+            message(Q3, g).start()
 
     def stats_forward(w):
         stat_message(w - 1).wait_recv()
@@ -204,14 +291,14 @@
     def turn(i, carry):
         at(i, -AHEAD, begin_queries)
         at(i, -AHEAD, begin_keys)
-        at(i, 0, functools.partial(forward, Q2))
+        at(i, 0, forward_first)
 
         @pl.when(i == 0)
         def _():
             stats_forward(1)
 
         at(i, 1, work_near)
-        at(i, 2, functools.partial(forward, Q3))
+        at(i, 2, forward_second)
 
         @pl.when(i == 2)
         def _():
@@ -222,8 +309,8 @@
             stat_message(2).wait_recv()
 
         at(i, 4, work_far)
-        at(i, 6, functools.partial(add_on, R2))
-        at(i, 8, functools.partial(add_on, R1))
+        at(i, 6, add_second)
+        at(i, 8, add_first)
         at(i, 10, finish)
         at(i, 12, settle)
         return carry
@@ -285,7 +372,7 @@
         scratch_shapes=[pltpu.VMEM((tokens, features), low)] * 5
         + [
             pltpu.VMEM((heads, tokens), wide),
-            pltpu.SemaphoreType.DMA((6,)),
+            pltpu.SemaphoreType.DMA((8,)),
             pltpu.VMEM((3, groups, BLOCK, width), low),
             pltpu.SemaphoreType.DMA((3, groups)),
             pltpu.VMEM((WINDOW, groups, 2, BLOCK, width), low),
@@ -303,6 +390,9 @@
             pltpu.SemaphoreType.DMA((KINDS, groups)),
             pltpu.SemaphoreType.DMA((WINDOW - 1,)),
             pltpu.SemaphoreType.DMA((WINDOW - 1,)),
+            pltpu.VMEM((groups, BLOCK, width), low),
+            pltpu.SemaphoreType.DMA((groups,)),
+            pltpu.SemaphoreType.DMA((groups,)),
         ],
         compiler_params=pltpu.CompilerParams(
             collective_id=0, has_side_effects=True, vmem_limit_bytes=62 * 1024 * 1024

time: 68.8 us -> 69.1 us (level)
  the two profiles are of different devices: /device:TPU:0 before, /device:TPU:1 now
where the time goes in v4:
time: 69.1 us; the launch traced here: 69 us
  Pallas kernels  68.3 us (99%)
    pallas_call x1, Pallas kernels, local(): pl.pallas_call(functools.partial(kernel, rows, cols, groups, heads), out_...  66.1 us
    pallas_call x1, Pallas kernels, local(): pl.pallas_call(store_kernel, out_shape=(out, out, out), in_specs=[hbm] *...  2.19 us

profile of v4, /device:TPU:1, one launch (start us, length us, event | category | flops | bytes accessed | tf_op | source)
XLA Modules:
  0.0 69.0 jit_solution(9514326421228667043)
XLA Ops:
  0.6 66.1 %block_sparse_backward.1 = (bf16[128,2048]{1,0:T(8,128)(2,1)}, bf16[128,2048]{1,0:T(8,128)(2,1)}, bf16[128,2048]{1,0:T(8,128)(2,1)}) custom-call(bf16[128,2048]{1,0:T(8,128)(2,1)} %q_hbm.1, bf16[128,2048]{1,0:T(8,128)(2,1)} %k_hbm.1, bf16[128,2048]{1,0:T(8,128)(2,1)} %v_hbm.1, bf16[128,2048]{1,0:T(8,128)(2,1)} %o_hbm.1, bf16[128,2048]{1,0:T(8,128)(2,1)} %do_hbm.1, ...), custom_call_target="tpu_custom_call" | custom-call | flops 2684354560 | bytes 4194304 | tf_op jit(solution)/shard_map/block_sparse_backward/pallas_call | solution.py:367
  66.8 2.2 %store_gradients.1 = (bf16[128,2048]{1,0:T(8,128)(2,1)}, bf16[128,2048]{1,0:T(8,128)(2,1)}, bf16[128,2048]{1,0:T(8,128)(2,1)}) custom-call(bf16[128,2048]{1,0:T(8,128)(2,1)} %get-tuple-element.6.a_ref, bf16[128,2048]{1,0:T(8,128)(2,1)} %get-tuple-element.7.b_ref, bf16[128,2048]{1,0:T(8,128)(2,1)} %get-tuple-element.8.c_ref), custom_call_target="tpu_custom_call" | custom-call | tf_op jit(solution)/shard_map/store_gradients/pallas_call | solution.py:407

commit v5 on v4

--- a/solution.py
+++ b/solution.py
@@ -290,7 +290,6 @@
 
     def turn(i, carry):
         at(i, -AHEAD, begin_queries)
-        at(i, -AHEAD, begin_keys)
         at(i, 0, forward_first)
 
         @pl.when(i == 0)
@@ -317,12 +316,20 @@
 
     for load in loads[:2]:
         load.wait()
-    for g in range(AHEAD):
+
+    def begin_some_queries(g, carry):
         begin_queries(g)
+        return carry
+
+    lax.fori_loop(0, AHEAD, begin_some_queries, 0)
     for load in loads[2:4]:
         load.wait()
-    for g in range(AHEAD):
+
+    def begin_all_keys(g, carry):
         begin_keys(g)
+        return carry
+
+    lax.fori_loop(0, groups, begin_all_keys, 0)
     for load in loads[4:]:
         load.wait()
     make_stats()

time: 69.1 us -> 69.1 us (level)
  no operation moved by 1% of the time
where the time goes in v5:
time: 69.1 us; the launch traced here: 69 us
  Pallas kernels  68.3 us (99%)
    pallas_call x1, Pallas kernels, local(): pl.pallas_call(functools.partial(kernel, rows, cols, groups, heads), out_...  66.1 us
    pallas_call x1, Pallas kernels, local(): pl.pallas_call(store_kernel, out_shape=(out, out, out), in_specs=[hbm] *...  2.19 us

profile of v5, /device:TPU:1, one launch (start us, length us, event | category | flops | bytes accessed | tf_op | source)
XLA Modules:
  0.0 69.0 jit_solution(10344557769033372070)
XLA Ops:
  0.6 66.1 %block_sparse_backward.1 = (bf16[128,2048]{1,0:T(8,128)(2,1)}, bf16[128,2048]{1,0:T(8,128)(2,1)}, bf16[128,2048]{1,0:T(8,128)(2,1)}) custom-call(bf16[128,2048]{1,0:T(8,128)(2,1)} %q_hbm.1, bf16[128,2048]{1,0:T(8,128)(2,1)} %k_hbm.1, bf16[128,2048]{1,0:T(8,128)(2,1)} %v_hbm.1, bf16[128,2048]{1,0:T(8,128)(2,1)} %o_hbm.1, bf16[128,2048]{1,0:T(8,128)(2,1)} %do_hbm.1, ...), custom_call_target="tpu_custom_call" | custom-call | flops 2684354560 | bytes 4194304 | tf_op jit(solution)/shard_map/block_sparse_backward/pallas_call | solution.py:374
  66.8 2.2 %store_gradients.1 = (bf16[128,2048]{1,0:T(8,128)(2,1)}, bf16[128,2048]{1,0:T(8,128)(2,1)}, bf16[128,2048]{1,0:T(8,128)(2,1)}) custom-call(bf16[128,2048]{1,0:T(8,128)(2,1)} %get-tuple-element.6.a_ref, bf16[128,2048]{1,0:T(8,128)(2,1)} %get-tuple-element.7.b_ref, bf16[128,2048]{1,0:T(8,128)(2,1)} %get-tuple-element.8.c_ref), custom_call_target="tpu_custom_call" | custom-call | tf_op jit(solution)/shard_map/store_gradients/pallas_call | solution.py:414

commit v6 on v5

--- a/solution.py
+++ b/solution.py
@@ -11,7 +11,8 @@
 HEAD_DIM = 128
 BLOCK = 128
 WINDOW = 4
-AHEAD = 8
+AHEAD = 4
+GROUP_HEADS = 2
 BIG = 1e30
 MESH = pl.DeviceIdType.MESH
 
@@ -32,7 +33,7 @@
     send_sem, recv_sem, stat_send, stat_recv, gq_leap, leap_send, leap_recv,
 ):
     inverse = 1.0 / math.sqrt(HEAD_DIM)
-    width = HEAD_DIM
+    width = GROUP_HEADS * HEAD_DIM
     r = lax.axis_index("pb")
     c = lax.axis_index("ka")
     right = (r, lax.rem(c + 1, cols))
@@ -157,41 +158,47 @@
                 blocked = (1 - adj_ref[0, a, 0, w]).astype(jnp.float32) * BIG
                 stats[0, pl.ds(2 * heads + a * WINDOW + w, 1), :] = jnp.full((1, BLOCK), blocked, jnp.float32)
 
-    def pair_terms(g, first):
+    def part(hh):
+        return slice(hh * HEAD_DIM, (hh + 1) * HEAD_DIM)
+
+    def pair_terms(g, hh, first):
+        h = g * GROUP_HEADS + hh
         pair = (first, first + 1)
         span = pl.ds(first * BLOCK, 2 * BLOCK)
-        kk = kvb[g, 0]
-        vv = kvb[g, 1]
-        qq = visit[first : first + 2, g, 0].reshape(2 * BLOCK, HEAD_DIM)
-        dd = visit[first : first + 2, g, 1].reshape(2 * BLOCK, HEAD_DIM)
-        delta = jnp.concatenate([stats[w, pl.ds(heads + g, 1), :] for w in pair], axis=1)
+        kk = kvb[g, 0, :, part(hh)]
+        vv = kvb[g, 1, :, part(hh)]
+        qq = visit[first : first + 2, g, 0, :, part(hh)].reshape(2 * BLOCK, HEAD_DIM)
+        dd = visit[first : first + 2, g, 1, :, part(hh)].reshape(2 * BLOCK, HEAD_DIM)
+        delta = jnp.concatenate([stats[w, pl.ds(heads + h, 1), :] for w in pair], axis=1)
         for a in range(2):
             norms = jnp.concatenate(
                 [
-                    stats[w, pl.ds(g, 1), :] + stats[w, pl.ds(2 * heads + a * WINDOW + w, 1), :]
+                    stats[w, pl.ds(h, 1), :] + stats[w, pl.ds(2 * heads + a * WINDOW + w, 1), :]
                     for w in pair
                 ],
                 axis=1,
             )
             half = slice(a * BLOCK, (a + 1) * BLOCK)
             prob = jnp.exp(dot(kk[half], qq, 1, 1) * inverse - norms)
-            probs[g, half, span] = prob.astype(jnp.bfloat16)
+            probs[h, half, span] = prob.astype(jnp.bfloat16)
             prob_grad = dot(vv[half], dd, 1, 1)
             score_grad = prob * (prob_grad - delta) * inverse
-            score_grads[g, half, span] = score_grad.astype(jnp.bfloat16)
-        return dot(score_grads[g, :, span], kk, 0, 0)
+            score_grads[h, half, span] = score_grad.astype(jnp.bfloat16)
+        return dot(score_grads[h, :, span], kk, 0, 0)
 
     def work_near(g):
         message(KV, g).wait_recv()
-        grad_q = pair_terms(g, 0)
-        gq_part[0, g] = grad_q[:BLOCK]
-        gq_part[1, g] = grad_q[BLOCK:]
+        for hh in range(GROUP_HEADS):
+            grad_q = pair_terms(g, hh, 0)
+            gq_part[0, g, :, part(hh)] = grad_q[:BLOCK]
+            gq_part[1, g, :, part(hh)] = grad_q[BLOCK:]
 
     def work_far(g):
         message(Q3, g).wait_recv()
-        grad_q = pair_terms(g, 2)
-        gq_part[2, g] = grad_q[:BLOCK]
-        gq_send[0, g] = grad_q[BLOCK:].astype(jnp.bfloat16)
+        for hh in range(GROUP_HEADS):
+            grad_q = pair_terms(g, hh, 2)
+            gq_part[2, g, :, part(hh)] = grad_q[:BLOCK]
+            gq_send[0, g, :, part(hh)] = grad_q[BLOCK:].astype(jnp.bfloat16)
 
         @pl.when(lands)
         def _():
@@ -201,11 +208,13 @@
         def _():
             message(R3, g).start()
 
-        qq = visit[:, g, 0].reshape(WINDOW * BLOCK, HEAD_DIM)
-        dd = visit[:, g, 1].reshape(WINDOW * BLOCK, HEAD_DIM)
-        for n, total in ((0, dot(score_grads[g], qq, 1, 0)), (1, dot(probs[g], dd, 1, 0))):
-            gkv_near[g, n] = total[:BLOCK]
-            gkv_send[g, n] = total[BLOCK:].astype(jnp.bfloat16)
+        for hh in range(GROUP_HEADS):
+            h = g * GROUP_HEADS + hh
+            qq = visit[:, g, 0, :, part(hh)].reshape(WINDOW * BLOCK, HEAD_DIM)
+            dd = visit[:, g, 1, :, part(hh)].reshape(WINDOW * BLOCK, HEAD_DIM)
+            for n, total in ((0, dot(score_grads[h], qq, 1, 0)), (1, dot(probs[h], dd, 1, 0))):
+                gkv_near[g, n, :, part(hh)] = total[:BLOCK]
+                gkv_send[g, n, :, part(hh)] = total[BLOCK:].astype(jnp.bfloat16)
         message(GKV, g).start()
 
     def add_second(g):
@@ -296,22 +305,23 @@
         def _():
             stats_forward(1)
 
+        at(i, 1, forward_second)
+
+        @pl.when(i == 1)
+        def _():
+            stats_forward(2)
+
         at(i, 1, work_near)
-        at(i, 2, forward_second)
-
-        @pl.when(i == 2)
-        def _():
-            stats_forward(2)
-
-        @pl.when(i == 4)
+
+        @pl.when(i == 3)
         def _():
             stat_message(2).wait_recv()
 
-        at(i, 4, work_far)
-        at(i, 6, add_second)
-        at(i, 8, add_first)
-        at(i, 10, finish)
-        at(i, 12, settle)
+        at(i, 3, work_far)
+        at(i, 4, add_second)
+        at(i, 5, add_first)
+        at(i, 6, finish)
+        at(i, 7, settle)
         return carry
 
     for load in loads[:2]:
@@ -335,7 +345,7 @@
     make_stats()
     stat_message(0).start()
 
-    lax.fori_loop(0, groups + 12, turn, 0)
+    lax.fori_loop(0, groups + 7, turn, 0)
 
     for w in range(WINDOW - 1):
         stat_message(w).wait_send()
@@ -365,8 +375,8 @@
 def local(rows, cols, queries, keys, values, outputs, d_out, row_lse, adjacency):
     tokens, features = queries.shape
     heads = features // HEAD_DIM
-    groups = heads
-    width = HEAD_DIM
+    groups = heads // GROUP_HEADS
+    width = GROUP_HEADS * HEAD_DIM
     low, wide = jnp.bfloat16, jnp.float32
     hbm = pl.BlockSpec(memory_space=pltpu.HBM)
     out = jax.ShapeDtypeStruct((tokens, features), low)
@@ -385,8 +395,8 @@
             pltpu.VMEM((WINDOW, groups, 2, BLOCK, width), low),
             pltpu.VMEM((groups, 2, 2 * BLOCK, width), low),
             pltpu.VMEM((WINDOW, 2 * heads + 2 * WINDOW, BLOCK), wide),
-            pltpu.VMEM((groups, 2 * BLOCK, WINDOW * BLOCK), low),
-            pltpu.VMEM((groups, 2 * BLOCK, WINDOW * BLOCK), low),
+            pltpu.VMEM((heads, 2 * BLOCK, WINDOW * BLOCK), low),
+            pltpu.VMEM((heads, 2 * BLOCK, WINDOW * BLOCK), low),
             pltpu.VMEM((WINDOW - 1, groups, BLOCK, width), wide),
             pltpu.VMEM((groups, 2, BLOCK, width), wide),
             pltpu.VMEM((WINDOW - 1, groups, BLOCK, width), low),

time: 69.1 us -> 66.5 us (0.962)
  the two profiles are of different devices: /device:TPU:1 before, /device:TPU:0 now
where the time goes in v6:
time: 66.5 us; the launch traced here: 66.4 us
  Pallas kernels  65.7 us (99%)
    pallas_call x1, Pallas kernels, local(): pl.pallas_call(functools.partial(kernel, rows, cols, groups, heads), out_...  63.5 us
    pallas_call x1, Pallas kernels, local(): pl.pallas_call(store_kernel, out_shape=(out, out, out), in_specs=[hbm] *...  2.19 us

profile of v6, /device:TPU:0, one launch (start us, length us, event | category | flops | bytes accessed | tf_op | source)
XLA Modules:
  0.0 66.4 jit_solution(14827058268877051256)
XLA Ops:
  0.6 63.5 %block_sparse_backward.1 = (bf16[128,2048]{1,0:T(8,128)(2,1)}, bf16[128,2048]{1,0:T(8,128)(2,1)}, bf16[128,2048]{1,0:T(8,128)(2,1)}) custom-call(bf16[128,2048]{1,0:T(8,128)(2,1)} %q_hbm.1, bf16[128,2048]{1,0:T(8,128)(2,1)} %k_hbm.1, bf16[128,2048]{1,0:T(8,128)(2,1)} %v_hbm.1, bf16[128,2048]{1,0:T(8,128)(2,1)} %o_hbm.1, bf16[128,2048]{1,0:T(8,128)(2,1)} %do_hbm.1, ...), custom_call_target="tpu_custom_call" | custom-call | flops 2684354560 | bytes 4194304 | tf_op jit(solution)/shard_map/block_sparse_backward/pallas_call | solution.py:384
  64.2 2.2 %store_gradients.1 = (bf16[128,2048]{1,0:T(8,128)(2,1)}, bf16[128,2048]{1,0:T(8,128)(2,1)}, bf16[128,2048]{1,0:T(8,128)(2,1)}) custom-call(bf16[128,2048]{1,0:T(8,128)(2,1)} %get-tuple-element.6.a_ref, bf16[128,2048]{1,0:T(8,128)(2,1)} %get-tuple-element.7.b_ref, bf16[128,2048]{1,0:T(8,128)(2,1)} %get-tuple-element.8.c_ref), custom_call_target="tpu_custom_call" | custom-call | tf_op jit(solution)/shard_map/store_gradients/pallas_call | solution.py:424

commit v7 on v6

--- a/solution.py
+++ b/solution.py
@@ -313,15 +313,15 @@
 
         at(i, 1, work_near)
 
-        @pl.when(i == 3)
+        @pl.when(i == 2)
         def _():
             stat_message(2).wait_recv()
 
-        at(i, 3, work_far)
-        at(i, 4, add_second)
-        at(i, 5, add_first)
-        at(i, 6, finish)
-        at(i, 7, settle)
+        at(i, 2, work_far)
+        at(i, 3, add_second)
+        at(i, 4, add_first)
+        at(i, 5, finish)
+        at(i, 6, settle)
         return carry
 
     for load in loads[:2]:
@@ -345,7 +345,7 @@
     make_stats()
     stat_message(0).start()
 
-    lax.fori_loop(0, groups + 7, turn, 0)
+    lax.fori_loop(0, groups + 6, turn, 0)
 
     for w in range(WINDOW - 1):
         stat_message(w).wait_send()

time: 66.5 us -> 67.6 us (1.017)
  Pallas kernels: 65.7 us -> 66.8 us
    pallas_call x1, Pallas kernels: 63.5 us -> 64.6 us  [local(): pl.pallas_call(functools.partial(kernel, rows, cols, groups, heads), out_...]
where the time goes in v7:
time: 67.6 us; the launch traced here: 67.4 us
  Pallas kernels  66.8 us (99%)
    pallas_call x1, Pallas kernels, local(): pl.pallas_call(functools.partial(kernel, rows, cols, groups, heads), out_...  64.6 us
    pallas_call x1, Pallas kernels, local(): pl.pallas_call(store_kernel, out_shape=(out, out, out), in_specs=[hbm] *...  2.19 us

profile of v7, /device:TPU:0, one launch (start us, length us, event | category | flops | bytes accessed | tf_op | source)
XLA Modules:
  0.0 67.4 jit_solution(8672605245150301110)
XLA Ops:
  0.6 64.6 %block_sparse_backward.1 = (bf16[128,2048]{1,0:T(8,128)(2,1)}, bf16[128,2048]{1,0:T(8,128)(2,1)}, bf16[128,2048]{1,0:T(8,128)(2,1)}) custom-call(bf16[128,2048]{1,0:T(8,128)(2,1)} %q_hbm.1, bf16[128,2048]{1,0:T(8,128)(2,1)} %k_hbm.1, bf16[128,2048]{1,0:T(8,128)(2,1)} %v_hbm.1, bf16[128,2048]{1,0:T(8,128)(2,1)} %o_hbm.1, bf16[128,2048]{1,0:T(8,128)(2,1)} %do_hbm.1, ...), custom_call_target="tpu_custom_call" | custom-call | flops 2684354560 | bytes 4194304 | tf_op jit(solution)/shard_map/block_sparse_backward/pallas_call | solution.py:384
  65.2 2.2 %store_gradients.1 = (bf16[128,2048]{1,0:T(8,128)(2,1)}, bf16[128,2048]{1,0:T(8,128)(2,1)}, bf16[128,2048]{1,0:T(8,128)(2,1)}) custom-call(bf16[128,2048]{1,0:T(8,128)(2,1)} %get-tuple-element.6.a_ref, bf16[128,2048]{1,0:T(8,128)(2,1)} %get-tuple-element.7.b_ref, bf16[128,2048]{1,0:T(8,128)(2,1)} %get-tuple-element.8.c_ref), custom_call_target="tpu_custom_call" | custom-call | tf_op jit(solution)/shard_map/store_gradients/pallas_call | solution.py:424
